TPU v7x, 32 devices: a whole 2x2x4 slice. The times are simulated.
32 devices in a mesh: lat: 4 (over y, x), lon: 8 (over z, core).
Axes of the slice: x: 2, y: 2, z: 4, core: 2. Of those that a mesh axis runs over, the one named last changes fastest.
Arguments:
- adjoint: float32 [16, 24, 64, 1024], P(None, None, 'lat', 'lon'), may hold values from -6 to 6
- courant: float32 [2, 24, 64, 1024], P(None, None, 'lat', 'lon'), may hold values from -0.35 to 0.35
- vert_diff: float32 [24], replicated, may hold values from 0.005 to 0.05
- kernel: float32 [24, 65536], P(None, ('lat', 'lon')), may hold values from 0.1 to 1
- innovation: float32 [65536], P(('lat', 'lon')), may hold values from -6 to 6
- sound_col: int32 [65536], P(('lat', 'lon')), may hold values from 0 to 65535, as said below
- sound_count: int32 [32], P(('lat', 'lon')), may hold values from 1024 to 2048, as said below
Outputs:
- adjoint_out: float32 [16, 24, 64, 1024], P(None, None, 'lat', 'lon')
Inputs may be any that keep to these rules, and one draw needn't show every extreme that they name: `sound_col`: of one device's slots, at most 128 go to grid columns of any one tile of 16 x 128 cells, and in every draw some device sends exactly 128 live soundings to one tile. `sound_count`: device 0 has all its slots live in every draw.
All inputs are finite; a program needn't handle non-finite values.
Results may differ from a plain program's by a relative error of at most 0.00002.
Values sent between devices are 32-bit elements; how exact they have to be, the bound alone decides.
A program may use at most 128 MiB of HBM per device.

v0:
```python
import jax
import jax.numpy as jnp
from jax import lax
from jax.sharding import PartitionSpec as P


def padded_2(cells, sides, width):
    for axis, dim in sides:
        count = lax.axis_size(axis)
        head = lax.slice_in_dim(cells, 0, width, axis=dim)
        tail = lax.slice_in_dim(cells, cells.shape[dim] - width, cells.shape[dim], axis=dim)
        cells = jnp.concatenate(
            [
                lax.ppermute(tail, axis, [(i, (i + 1) % count) for i in range(count)]),
                cells,
                lax.ppermute(head, axis, [((i + 1) % count, i) for i in range(count)]),
            ],
            axis=dim,
        )
    return cells


def advance(padded, winds, vert_diff):
    centre = padded[:, :, 1:-1, 1:-1]
    north = padded[:, :, 2:, 1:-1]
    south = padded[:, :, :-2, 1:-1]
    east = padded[:, :, 1:-1, 2:]
    west = padded[:, :, 1:-1, :-2]
    upper = jnp.concatenate([centre[:, 1:], centre[:, -1:]], axis=1)
    lower = jnp.concatenate([centre[:, :1], centre[:, :-1]], axis=1)
    along = winds[0]
    across = winds[1]
    result = (
        centre
        + jnp.maximum(along, 0.0) * (east - centre)
        + jnp.maximum(-along, 0.0) * (west - centre)
    )
    result = (
        result
        + jnp.maximum(across, 0.0) * (north - centre)
        + jnp.maximum(-across, 0.0) * (south - centre)
    )
    result = result + 0.05 * (east + west + north + south - 4.0 * centre)
    return result + vert_diff[:, None, None] * (upper + lower - 2.0 * centre)


def row_mask(rows_tile, width):
    first = lax.axis_index("lat") * rows_tile - width
    rows = first + jnp.arange(rows_tile + 2 * width, dtype=jnp.int32)
    inside = (rows >= 0) & (rows < rows_tile * lax.axis_size("lat"))
    return inside.astype(jnp.float32)[:, None]


def per_device(adjoint, courant, vert_diff, kernel, innovation, sound_col, sound_count):
    tracers, levels, rows_tile, cols_tile = adjoint.shape
    lat_tiles = lax.axis_size("lat")
    lon_tiles = lax.axis_size("lon")
    devices_all = lat_tiles * lon_tiles
    slots = sound_col.shape[0]
    per_tile = 2 * slots // devices_all
    ncell = rows_tile * cols_tile
    grid_cols = cols_tile * lon_tiles
    grid_row = sound_col // grid_cols
    grid_col = sound_col % grid_cols
    tile = grid_row // rows_tile * lon_tiles + grid_col // cols_tile
    cell = grid_row % rows_tile * cols_tile + grid_col % cols_tile
    live = jnp.arange(slots, dtype=jnp.int32) < sound_count[0]
    onehot = (
        (tile[:, None] == jnp.arange(devices_all, dtype=jnp.int32)[None, :]) & live[:, None]
    ).astype(jnp.int32)
    rank = jnp.sum(jnp.cumsum(onehot, axis=0) * onehot, axis=1) - 1
    target = jnp.where(live, tile * per_tile + rank, devices_all * per_tile)
    payload = kernel * innovation[None, :]
    packed = (
        jnp.zeros((levels, devices_all * per_tile), jnp.float32)
        .at[:, target]
        .set(payload, mode="drop")
    )
    places = (
        jnp.full((devices_all * per_tile,), -1.0, jnp.float32)
        .at[target]
        .set(cell.astype(jnp.float32), mode="drop")
    )
    received, sources = (
        lax.all_to_all(
            packed.reshape(levels, devices_all, per_tile),
            ("lat", "lon"),
            split_axis=1,
            concat_axis=1,
            tiled=True,
        ),
        lax.all_to_all(
            places.reshape(1, devices_all, per_tile),
            ("lat", "lon"),
            split_axis=1,
            concat_axis=1,
            tiled=True,
        ),
    )
    received = received.reshape(levels, devices_all * per_tile)
    sources = sources.reshape(devices_all * per_tile)
    index = jnp.where(sources < 0.0, ncell, sources.astype(jnp.int32))
    forcing = jnp.zeros((levels, ncell), jnp.float32).at[:, index].add(received, mode="drop")
    forcing = forcing.reshape(levels, rows_tile, cols_tile)

    def single_step(field):
        padded = padded_2(field, (("lat", 2), ("lon", 3)), 1) * row_mask(rows_tile, 1)
        return advance(padded, courant, vert_diff)

    middle = single_step(adjoint) + forcing[None]
    return single_step(middle)


def solution(mesh):
    placed = (
        P(None, None, "lat", "lon"),
        P(None, None, "lat", "lon"),
        P(),
        P(None, ("lat", "lon")),
        P(("lat", "lon")),
        P(("lat", "lon")),
        P(("lat", "lon")),
    )
    return jax.shard_map(
        per_device,
        mesh=mesh,
        in_specs=placed,
        out_specs=P(None, None, "lat", "lon"),
        check_vma=False,
    )
```

profile of v0, /device:TPU:0, one launch (start us, length us, event | category | flops | bytes accessed | tf_op | source)
XLA Modules:
  0.0 220.9 jit_solution(7687495209640322737)
XLA Ops:
  0.0 3.1 %fusion.37 = (f32[16,24,1,128]{3,2,1,0:T(1,128)}, f32[16,24,1,128]{3,2,1,0:T(1,128)}) fusion(f32[16,24,16,128]{3,2,1,0:T(8,128)} %param.7), kind=kLoop, calls=%fused_computation.80 | loop fusion | bytes 786432 | tf_op jit(solution)/shard_map/slice | solution.py:11
  3.1 3.9 %collective-permute-start.1 = (f32[16,24,1,128]{3,1,2,0:T(8,128)}, f32[16,24,1,128]{3,1,2,0:T(8,128)}, u32[]{:S(2)}, u32[]{:S(2)}) collective-permute-start(f32[16,24,1,128]{3,1,2,0:T(8,128)} %bitcast.17), channel_id=1, source_target_pairs={{8,0},{16,8},{24,16},{0,24},{9,1},{17,9},{25,17},{1,25},{10,2},{18... | collective-permute-start | bytes 589832 | tf_op jit(solution)/shard_map/ppermute | solution.py:16
  8.4 0.7 fusion.15
  9.1 15.9 %reduce-window.6 = s32[32,16,128]{2,1,0:T(8,128)S(1)} reduce-window(s32[32,16,128]{2,1,0:T(8,128)} %fusion.15, s32[]{:T(128)} %constant.91.clone.1), window={size=1x1x128 pad=0_0x0_0x127_0}, to_apply=%region_0.1 | reduce-window | flops 8323072 | bytes 524292 | tf_op jit(solution)/shard_map/reduce-window
  25.0 0.8 slice.141
  25.8 1.2 copy.111
  27.5 8.6 %scatter_custom_fusion = f32[4096]{0:T(1024)} fusion(s32[2048]{0:T(1024)S(1)} %compare_select_fusion.2, f32[2048]{0:T(1024)S(1)} %get-tuple-element.25, f32[]{:T(128)} %constant.97.clone.1), kind=kCustom, calls=%fused_computation.64 | custom fusion | bytes 16388 | tf_op jit(solution)/shard_map/scatter | solution.py:82
  36.1 6.3 %all-to-all-start = ((f32[1,32,128]{2,0,1:T(1,128)}), f32[1,32,128]{2,0,1:T(1,128)S(1)}, u32[]{:S(2)}, u32[]{:S(2)}) async-start(f32[1,32,128]{2,0,1:T(1,128)} %bitcast.9), calls=%async_computation | async-start | bytes 32768 | tf_op jit(solution)/shard_map/all_to_all | solution.py:92
  42.5 1.6 multiply_bitcast_fusion
  44.1 1.8 maximum_bitcast_fusion.3
  46.0 7.9 %copy.90 = f32[16,24,16,128]{1,0,3,2:T(8,128)} copy(f32[16,24,16,128]{3,2,1,0:T(8,128)S(1)} %copy-done.2) | data formatting | bytes 6291456 | tf_op args[0]
  53.8 1.3 copy.101
  55.1 6.2 %scatter_custom_fusion.1 = f32[24,4096]{0,1:T(8,128)S(1)} fusion(s32[2048]{0:T(1024)} %copy-done.10, f32[2048,24]{1,0:T(8,128)S(1)} %copy.101, f32[]{:T(128)} %constant.93.clone.1), kind=kCustom, calls=%fused_computation.16 | custom fusion | bytes 393728 | tf_op jit(solution)/shard_map/scatter | solution.py:77
  61.3 1.3 copy.102
  62.6 1.7 copy.98
  64.3 1.7 copy.97
  66.0 0.7 copy.96
  68.0 1.4 copy.91
  69.4 1.4 copy.89
  70.8 6.8 %pad_maximum_fusion = f32[16,24,18,128]{1,0,3,2:T(8,128)S(1)} fusion(f32[16,24,1,128]{1,0,3,2:T(8,128)S(1)} %copy.91, f32[16,24,16,128]{1,0,3,2:T(8,128)} %copy.90, f32[16,24,1,128]{1,0,3,2:T(8,128)S(1)} %copy.89), kind=kLoop, calls=%fused_computation.3 | loop fusion | flops 1769472 | bytes 7077888 | tf_op jit(solution)/shard_map/concatenate | solution.py:12
  77.7 6.5 %copy-done.1 = f32[16,24,18,128]{1,0,3,2:T(8,128)} copy-done((f32[16,24,18,128]{1,0,3,2:T(8,128)}, f32[16,24,18,128]{1,0,3,2:T(8,128)S(1)}, u32[]{:S(2)}) %copy-start.1) | copy-done | bytes 3538968
  84.8 3.4 %collective-permute-start.3 = (f32[16,24,18,1]{1,0,3,2:T(8,128)S(1)}, f32[16,24,18,1]{1,0,3,2:T(8,128)}, u32[]{:S(2)}, u32[]{:S(2)}) collective-permute-start(f32[16,24,18,1]{1,0,3,2:T(8,128)S(1)} %get-tuple-element.6), channel_id=1, source_target_pairs={{1,0},{2,1},{3,2},{4,3},{5,4},{6,5},{7,6},{0,7},{9,8},{10,9},{11,1... | collective-permute-start | bytes 82952 | tf_op jit(solution)/shard_map/ppermute | solution.py:16
  88.2 6.0 %all-to-all-start.1 = ((f32[24,32,128]{2,0,1:T(8,128)}), f32[24,32,128]{2,0,1:T(8,128)}, u32[]{:S(2)}, u32[]{:S(2)}) async-start(f32[24,32,128]{2,0,1:T(8,128)} %copy.102), calls=%async_computation.1 | async-start | bytes 786432 | tf_op jit(solution)/shard_map/all_to_all | solution.py:85
  94.9 12.2 %copy.93 = f32[16,24,18,128]{3,1,2,0:T(8,128)} copy(f32[16,24,18,128]{1,0,3,2:T(8,128)} %copy-done.1) | data formatting | bytes 7077888 | tf_op jit(solution)/shard_map/concatenate | solution.py:12
  107.1 2.7 %copy.94 = f32[16,24,18,1]{3,1,2,0:T(8,128)S(1)} copy(f32[16,24,18,1]{1,0,3,2:T(8,128)} %collective-permute-done.3) | data formatting | bytes 55296 | tf_op jit(solution)/shard_map/ppermute | solution.py:16
  109.8 3.9 %copy.92 = f32[16,24,18,1]{3,1,2,0:T(8,128)} copy(f32[16,24,18,1]{1,0,3,2:T(8,128)} %collective-permute-done.2) | data formatting | bytes 55296 | tf_op jit(solution)/shard_map/ppermute | solution.py:14
  113.7 5.4 %maximum_multiply_fusion = f32[16,24,18,130]{3,1,2,0:T(8,128)S(1)} fusion(f32[16,24,18,1]{3,1,2,0:T(8,128)S(1)} %copy.94, f32[16,24,18,128]{3,1,2,0:T(8,128)} %copy.93, f32[16,24,18,1]{3,1,2,0:T(8,128)} %copy.92, f32[18]{0:T(128)S(1)} %copy-done.11), kind=kLoop, calls=%fused_computation.4 | loop fusion | flops 2695680 | bytes 7188552 | tf_op jit(solution)/shard_map/mul | solution.py:107
  119.1 1.8 fusion.33
  120.9 1.2 copy-done
  122.1 4.4 %fusion.34 = (f32[16,23,16,128]{3,1,2,0:T(8,128)}, f32[16,23,16,128]{3,1,2,0:T(8,128)}) fusion(f32[16,24,18,130]{3,1,2,0:T(8,128)S(1)} %maximum_multiply_fusion), kind=kLoop, calls=%fused_computation.77 | loop fusion | bytes 12058624 | tf_op jit(solution)/shard_map/slice | solution.py:30
  126.5 1.1 bitcast_bitcast_fusion
  128.2 22.7 %scatter_custom_fusion.2 = f32[24,2048]{0,1:T(8,128)S(1)} fusion(s32[4096]{0:T(1024)} %bitcast.54, f32[4096,24]{1,0:T(8,128)S(1)} %copy.104, f32[]{:T(128)} %constant.93.clone.1), kind=kCustom, calls=%fused_computation.18 | custom fusion | flops 98304 | bytes 197120 | tf_op jit(solution)/shard_map/scatter-add | solution.py:103
  150.9 1.0 copy.105
  151.9 13.1 %fusion.3 = f32[16,24,16,128]{3,1,2,0:T(8,128)S(1)} fusion(f32[16,1,16,128]{3,1,2,0:T(1,128)} %get-tuple-element.12, f32[16,23,16,128]{3,1,2,0:T(8,128)} %get-tuple-element.14, f32[16,23,16,128]{3,1,2,0:T(8,128)} %get-tuple-element.13, f32[16,1,16,128]{3,1,2,0:T(1,128)} %get-tuple-element.11, f32[16,24,18,130]{3,1,2,0:T(8,128)} %copy-done, ...), kind=kLoop, calls=%fused_computation.11 | loop fusion | flops 21233664 | bytes 26148960 | tf_op jit(solution)/shard_map/add | solution.py:110
  165.0 2.5 %collective-permute-start.5 = (f32[16,24,1,128]{3,1,2,0:T(8,128)S(1)}, f32[16,24,1,128]{3,1,2,0:T(8,128)S(1)}, u32[]{:S(2)}, u32[]{:S(2)}) collective-permute-start(f32[16,24,1,128]{3,1,2,0:T(8,128)S(1)} %get-tuple-element.18), channel_id=1, source_target_pairs={{8,0},{16,8},{24,16},{0,24},{9,1},{17,9},{25,17},{1,25},{10,2},{18... | collective-permute-start | bytes 589832 | tf_op jit(solution)/shard_map/ppermute | solution.py:16
  167.5 5.3 %collective-permute-done.5 = f32[16,24,1,128]{3,1,2,0:T(8,128)S(1)} collective-permute-done((f32[16,24,1,128]{3,1,2,0:T(8,128)S(1)}, f32[16,24,1,128]{3,1,2,0:T(8,128)S(1)}, u32[]{:S(2)}, u32[]{:S(2)}) %collective-permute-start.5) | collective-permute-done | bytes 196640 | tf_op jit(solution)/shard_map/ppermute | solution.py:16
  172.9 4.4 %collective-permute-done.4 = f32[16,24,1,128]{3,1,2,0:T(8,128)S(1)} collective-permute-done((f32[16,24,1,128]{3,1,2,0:T(8,128)S(1)}, f32[16,24,1,128]{3,1,2,0:T(8,128)S(1)}, u32[]{:S(2)}, u32[]{:S(2)}) %collective-permute-start.4) | collective-permute-done | bytes 196640 | tf_op jit(solution)/shard_map/ppermute | solution.py:14
  178.2 4.0 %fusion.35 = (f32[16,24,18,1]{3,1,2,0:T(8,128)}, f32[16,24,18,1]{3,1,2,0:T(8,128)}) fusion(f32[16,24,18,128]{3,1,2,0:T(8,128)S(1)} %pad_maximum_fusion.1), kind=kLoop, calls=%fused_computation.78 | loop fusion | bytes 110592 | tf_op jit(solution)/shard_map/slice | solution.py:11
  182.1 3.9 %copy.115 = f32[16,24,18,1]{1,0,3,2:T(8,128)} copy(f32[16,24,18,1]{3,1,2,0:T(8,128)} %get-tuple-element.16) | data formatting | bytes 55296
  186.1 2.3 %collective-permute-start.7 = (f32[16,24,18,1]{1,0,3,2:T(8,128)}, f32[16,24,18,1]{1,0,3,2:T(8,128)}, u32[]{:S(2)}, u32[]{:S(2)}) collective-permute-start(f32[16,24,18,1]{1,0,3,2:T(8,128)} %copy.115), channel_id=1, source_target_pairs={{1,0},{2,1},{3,2},{4,3},{5,4},{6,5},{7,6},{0,7},{9,8},{10,9},{11,1... | collective-permute-start | bytes 82952 | tf_op jit(solution)/shard_map/ppermute | solution.py:16
  188.3 3.9 %copy.114 = f32[16,24,18,1]{1,0,3,2:T(8,128)} copy(f32[16,24,18,1]{3,1,2,0:T(8,128)} %get-tuple-element.15) | data formatting | bytes 55296
  192.3 3.9 %copy.109 = f32[16,24,18,1]{3,1,2,0:T(8,128)} copy(f32[16,24,18,1]{1,0,3,2:T(8,128)} %collective-permute-done.7) | data formatting | bytes 55296 | tf_op jit(solution)/shard_map/ppermute | solution.py:16
  196.2 2.7 %collective-permute-done.6 = f32[16,24,18,1]{1,0,3,2:T(8,128)} collective-permute-done((f32[16,24,18,1]{1,0,3,2:T(8,128)}, f32[16,24,18,1]{1,0,3,2:T(8,128)}, u32[]{:S(2)}, u32[]{:S(2)}) %collective-permute-start.6) | collective-permute-done | bytes 27680 | tf_op jit(solution)/shard_map/ppermute | solution.py:14
  198.9 4.0 %copy.108 = f32[16,24,18,1]{3,1,2,0:T(8,128)} copy(f32[16,24,18,1]{1,0,3,2:T(8,128)} %collective-permute-done.6) | data formatting | bytes 55296 | tf_op jit(solution)/shard_map/ppermute | solution.py:14
  202.9 6.4 %maximum_multiply_fusion.1 = f32[16,24,18,130]{3,1,2,0:T(8,128)S(1)} fusion(f32[16,24,18,1]{3,1,2,0:T(8,128)} %copy.109, f32[16,24,1,128]{3,1,2,0:T(8,128)} %copy-done.7, f32[16,24,16,128]{3,1,2,0:T(8,128)S(1)} %fusion.3, f32[16,24,1,128]{3,1,2,0:T(8,128)} %copy-done.8, f32[16,24,18,1]{3,1,2,0:T(8,128)} %copy.108, f32[18]{0:T(128)S(1)} %copy-done.11), kind=kLoop, calls=%fused_computation.5 | loop fusion | flops 4492800 | bytes 7188552 | tf_op jit(solution)/shard_map/mul | solution.py:107
  209.9 3.3 %fusion.32 = (f32[16,23,16,128]{3,1,2,0:T(8,128)S(1)}, f32[16,23,16,128]{3,1,2,0:T(8,128)}) fusion(f32[16,24,18,130]{3,1,2,0:T(8,128)S(1)} %maximum_multiply_fusion.1), kind=kLoop, calls=%fused_computation.75 | loop fusion | bytes 12058624 | tf_op jit(solution)/shard_map/slice | solution.py:30
  213.3 5.4 %fusion.6 = f32[16,24,16,128]{3,1,2,0:T(8,128)S(1)} fusion(f32[16,1,16,128]{3,1,2,0:T(1,128)S(1)} %get-tuple-element.8, f32[16,23,16,128]{3,1,2,0:T(8,128)} %get-tuple-element.10, f32[16,23,16,128]{3,1,2,0:T(8,128)S(1)} %get-tuple-element.9, f32[16,1,16,128]{3,1,2,0:T(1,128)S(1)} %get-tuple-element.7, f32[16,24,18,130]{3,1,2,0:T(8,128)S(1)} %maximum_multiply_fusion.1, ...), kind=kLoop, calls=%fused_computation.15 | loop fusion | flops 20447232 | bytes 25952352 | tf_op jit(solution)/shard_map/add | solution.py:44
  218.6 2.2 %copy.110 = f32[16,24,16,128]{3,2,1,0:T(8,128)} copy(f32[16,24,16,128]{3,1,2,0:T(8,128)S(1)} %fusion.6) | data formatting | bytes 6291456 | tf_op jit(solution)/shard_map/add | solution.py:44
  (50 shorter events, 6.0 us)
Async XLA Ops:
  0.0 46.0 %copy-start.2 = (f32[16,24,16,128]{3,2,1,0:T(8,128)S(1)}, f32[16,24,16,128]{3,2,1,0:T(8,128)}, u32[]{:S(2)}) copy-start(f32[16,24,16,128]{3,2,1,0:T(8,128)} %param.7) | copy-start | bytes 9437188
  0.0 42.5 %copy-start.9 = (f32[2048]{0:T(1024)S(1)}, f32[2048]{0:T(1024)}, u32[]{:S(2)}) copy-start(f32[2048]{0:T(1024)} %param.11) | copy-start | bytes 24580
  3.1 64.9 %collective-permute-start.1 = (f32[16,24,1,128]{3,1,2,0:T(8,128)}, f32[16,24,1,128]{3,1,2,0:T(8,128)}, u32[]{:S(2)}, u32[]{:S(2)}) collective-permute-start(f32[16,24,1,128]{3,1,2,0:T(8,128)} %bitcast.17), channel_id=1, source_target_pairs={{8,0},{16,8},{24,16},{0,24},{9,1},{17,9},{25,17},{1,25},{10,2},{18... | collective-permute-start | bytes 589832 | tf_op jit(solution)/shard_map/ppermute | solution.py:16
  7.0 62.4 %collective-permute-start = (f32[16,24,1,128]{3,1,2,0:T(8,128)}, f32[16,24,1,128]{3,1,2,0:T(8,128)}, u32[]{:S(2)}, u32[]{:S(2)}) collective-permute-start(f32[16,24,1,128]{3,1,2,0:T(8,128)} %bitcast.16), channel_id=1, source_target_pairs={{0,8},{8,16},{16,24},{24,0},{1,9},{9,17},{17,25},{25,1},{2,10},{10... | collective-permute-start | bytes 589832 | tf_op jit(solution)/shard_map/ppermute | solution.py:14
  27.5 15.0 %copy-start.10 = (s32[2048]{0:T(1024)}, s32[2048]{0:T(1024)S(1)}, u32[]{:S(2)}) copy-start(s32[2048]{0:T(1024)S(1)} %compare_select_fusion.2) | copy-start | bytes 24580
  36.1 52.1 %all-to-all-start = ((f32[1,32,128]{2,0,1:T(1,128)}), f32[1,32,128]{2,0,1:T(1,128)S(1)}, u32[]{:S(2)}, u32[]{:S(2)}) async-start(f32[1,32,128]{2,0,1:T(1,128)} %bitcast.9), calls=%async_computation | async-start | bytes 32768 | tf_op jit(solution)/shard_map/all_to_all | solution.py:92
  77.6 6.5 %copy-start.1 = (f32[16,24,18,128]{1,0,3,2:T(8,128)}, f32[16,24,18,128]{1,0,3,2:T(8,128)S(1)}, u32[]{:S(2)}) copy-start(f32[16,24,18,128]{1,0,3,2:T(8,128)S(1)} %pad_maximum_fusion) | copy-start | bytes 10616836
  84.8 22.2 %collective-permute-start.3 = (f32[16,24,18,1]{1,0,3,2:T(8,128)S(1)}, f32[16,24,18,1]{1,0,3,2:T(8,128)}, u32[]{:S(2)}, u32[]{:S(2)}) collective-permute-start(f32[16,24,18,1]{1,0,3,2:T(8,128)S(1)} %get-tuple-element.6), channel_id=1, source_target_pairs={{1,0},{2,1},{3,2},{4,3},{5,4},{6,5},{7,6},{0,7},{9,8},{10,9},{11,1... | collective-permute-start | bytes 82952 | tf_op jit(solution)/shard_map/ppermute | solution.py:16
  88.2 21.6 %collective-permute-start.2 = (f32[16,24,18,1]{1,0,3,2:T(8,128)}, f32[16,24,18,1]{1,0,3,2:T(8,128)}, u32[]{:S(2)}, u32[]{:S(2)}) collective-permute-start(f32[16,24,18,1]{1,0,3,2:T(8,128)} %get-tuple-element.5), channel_id=1, source_target_pairs={{0,1},{1,2},{2,3},{3,4},{4,5},{5,6},{6,7},{7,0},{8,9},{9,10},{10,1... | collective-permute-start | bytes 82952 | tf_op jit(solution)/shard_map/ppermute | solution.py:14
  88.2 38.3 %all-to-all-start.1 = ((f32[24,32,128]{2,0,1:T(8,128)}), f32[24,32,128]{2,0,1:T(8,128)}, u32[]{:S(2)}, u32[]{:S(2)}) async-start(f32[24,32,128]{2,0,1:T(8,128)} %copy.102), calls=%async_computation.1 | async-start | bytes 786432 | tf_op jit(solution)/shard_map/all_to_all | solution.py:85
  107.1 6.7 %copy-start.11 = (f32[18]{0:T(128)S(1)}, f32[18]{0:T(128)}, u32[]{:S(2)}) copy-start(f32[18]{0:T(128)} %and_convert_fusion) | copy-start | bytes 220
  119.1 3.0 %copy-start = (f32[16,24,18,130]{3,1,2,0:T(8,128)}, f32[16,24,18,130]{3,1,2,0:T(8,128)S(1)}, u32[]{:S(2)}) copy-start(f32[16,24,18,130]{3,1,2,0:T(8,128)S(1)} %maximum_multiply_fusion) | copy-start | bytes 10782724
  126.5 25.4 %copy-start.3 = (f32[24,16,128]{2,0,1:T(8,128)S(1)}, f32[24,16,128]{2,0,1:T(8,128)}, u32[]{:S(2)}) copy-start(f32[24,16,128]{2,0,1:T(8,128)} %copy.98) | copy-start | bytes 589828
  126.5 25.4 %copy-start.4 = (f32[24,16,128]{2,0,1:T(8,128)S(1)}, f32[24,16,128]{2,0,1:T(8,128)}, u32[]{:S(2)}) copy-start(f32[24,16,128]{2,0,1:T(8,128)} %copy.97) | copy-start | bytes 589828
  126.5 25.4 %copy-start.12 = (f32[24]{0:T(128)S(1)}, f32[24]{0:T(128)}, u32[]{:S(2)}) copy-start(f32[24]{0:T(128)} %param.9) | copy-start | bytes 292
  165.0 7.8 %collective-permute-start.5 = (f32[16,24,1,128]{3,1,2,0:T(8,128)S(1)}, f32[16,24,1,128]{3,1,2,0:T(8,128)S(1)}, u32[]{:S(2)}, u32[]{:S(2)}) collective-permute-start(f32[16,24,1,128]{3,1,2,0:T(8,128)S(1)} %get-tuple-element.18), channel_id=1, source_target_pairs={{8,0},{16,8},{24,16},{0,24},{9,1},{17,9},{25,17},{1,25},{10,2},{18... | collective-permute-start | bytes 589832 | tf_op jit(solution)/shard_map/ppermute | solution.py:16
  167.5 9.7 %collective-permute-start.4 = (f32[16,24,1,128]{3,1,2,0:T(8,128)S(1)}, f32[16,24,1,128]{3,1,2,0:T(8,128)S(1)}, u32[]{:S(2)}, u32[]{:S(2)}) collective-permute-start(f32[16,24,1,128]{3,1,2,0:T(8,128)S(1)} %get-tuple-element.17), channel_id=1, source_target_pairs={{0,8},{8,16},{16,24},{24,0},{1,9},{9,17},{17,25},{25,1},{2,10},{10... | collective-permute-start | bytes 589832 | tf_op jit(solution)/shard_map/ppermute | solution.py:14
  172.9 4.4 %copy-start.7 = (f32[16,24,1,128]{3,1,2,0:T(8,128)}, f32[16,24,1,128]{3,1,2,0:T(8,128)S(1)}, u32[]{:S(2)}) copy-start(f32[16,24,1,128]{3,1,2,0:T(8,128)S(1)} %collective-permute-done.5) | copy-start | bytes 589828
  177.2 0.7 copy-start.8
  186.1 6.2 %collective-permute-start.7 = (f32[16,24,18,1]{1,0,3,2:T(8,128)}, f32[16,24,18,1]{1,0,3,2:T(8,128)}, u32[]{:S(2)}, u32[]{:S(2)}) collective-permute-start(f32[16,24,18,1]{1,0,3,2:T(8,128)} %copy.115), channel_id=1, source_target_pairs={{1,0},{2,1},{3,2},{4,3},{5,4},{6,5},{7,6},{0,7},{9,8},{10,9},{11,1... | collective-permute-start | bytes 82952 | tf_op jit(solution)/shard_map/ppermute | solution.py:16
  192.3 6.7 %collective-permute-start.6 = (f32[16,24,18,1]{1,0,3,2:T(8,128)}, f32[16,24,18,1]{1,0,3,2:T(8,128)}, u32[]{:S(2)}, u32[]{:S(2)}) collective-permute-start(f32[16,24,18,1]{1,0,3,2:T(8,128)} %copy.114), channel_id=1, source_target_pairs={{0,1},{1,2},{2,3},{3,4},{4,5},{5,6},{6,7},{7,0},{8,9},{9,10},{10,1... | collective-permute-start | bytes 82952 | tf_op jit(solution)/shard_map/ppermute | solution.py:14
  209.9 3.4 %copy-start.5 = (f32[24,16,128]{2,0,1:T(8,128)S(1)}, f32[24,16,128]{2,0,1:T(8,128)}, u32[]{:S(2)}) copy-start(f32[24,16,128]{2,0,1:T(8,128)} %copy.96) | copy-start | bytes 589828
  209.9 3.3 %copy-start.6 = (f32[24,16,128]{2,0,1:T(8,128)S(1)}, f32[24,16,128]{2,0,1:T(8,128)}, u32[]{:S(2)}) copy-start(f32[24,16,128]{2,0,1:T(8,128)} %copy.95) | copy-start | bytes 589828
where the time goes:
time: 223 us; the launch traced here: 221 us
  local copies, waits for them, and re-layouts  101 us (45%)
  other arithmetic  82.5 us (37%)
  starting transfers between devices  24.4 us (11%)
  waiting for transfers between devices  12.5 us (6%)
    unnamed x29, local copies, waits for them, and re-layouts  24.1 us
    scatter-add x1, other arithmetic, per_device(): jnp.zeros((levels, ncell), jnp.float32).at[:, index]  22.7 us
    another operation x3, other arithmetic  16.2 us
    add x1, other arithmetic, per_device(): middle = single_step(adjoint) + forcing[None]  13.1 us
    concatenate x1, local copies, waits for them, and re-layouts, padded_2(): jnp.concatenate([lax.ppermute(tail, axis, [(i, (i + 1) % count) for i in...  12.2 us
    ppermute x4, starting transfers between devices, padded_2(): lax.ppermute(head, axis, [((i + 1) % count, i) for i in range(count)])  12 us
    mul x2, other arithmetic, single_step(): padded_2(field, (('lat', 2), ('lon', 3)), 1) * row_mask(rows_tile, 1)  11.8 us
    slice x4, local copies, waits for them, and re-layouts, advance(): lower = jnp.concatenate([centre[:, :1], centre[:, :-1]], axis=1)  10.1 us
  transfers between devices with their start and end apart: 10, of which 3 were waited for; matrix products, arithmetic and copies ran while one was open for 47% of the time, Pallas kernels for 0%

commit v1 on v0

v1 whole, which is shorter than its diff:
```python
import functools

import jax
import jax.numpy as jnp
from jax import lax
from jax.experimental import pallas as pl
from jax.experimental.pallas import tpu as pltpu
from jax.sharding import PartitionSpec as P

MESH = pl.DeviceIdType.MESH
F32 = jnp.float32
BF16 = jnp.bfloat16
GROUP = 4
BLOCK = 8
WIDE = 128
PAY = 32
TOP = 8


def kernel_body(
    lat_n, lon_n, tracers, levels, rows,
    adj, cour, kern, vd, count, innov, cols,
    out, sf,
    q0, q1, fq, wind, coef, kbuf, pbuf, send, recv, a_hi, a_lo, b_hi, b_lo,
    rank_hot, tile_ref, edge, edge_e, edge_w, halo, fedge, fedge_e, fedge_w, obuf,
    load_sem, row_send, row_recv, col_send, col_recv, pay_send, pay_recv,
    f_send, f_recv, out_sem, own_sem,
):
    la = lax.axis_index("lat")
    lo = lax.axis_index("lon")
    me = la * lon_n + lo
    total = lat_n * lon_n
    chunks = tracers // GROUP
    parts = levels // BLOCK
    slots = kern.shape[1]
    pieces = slots // WIDE
    east = lax.rem(lo + 1, lon_n)
    west = lax.rem(lo + lon_n - 1, lon_n)

    barrier = pltpu.get_barrier_semaphore()

    @pl.loop(1, total)
    def _(i):
        p = lax.rem(me + i, total)
        pl.semaphore_signal(
            barrier, inc=1, device_id=(p // lon_n, lax.rem(p, lon_n)), device_id_type=MESH
        )

    kload = pltpu.make_async_copy(kern, kbuf, load_sem.at[0])
    kload.start()
    loads = []
    for g in range(chunks):
        loads.append(
            pltpu.make_async_copy(
                adj.at[pl.ds(g * GROUP, GROUP)],
                q0.at[pl.ds(g * GROUP, GROUP), :, pl.ds(TOP, rows), :],
                load_sem.at[2 + g],
            )
        )
        loads[-1].start()
    wload = pltpu.make_async_copy(cour, wind, load_sem.at[1])
    wload.start()

    col = cols[...]
    grid_cols = lon_n * 128
    grid_row = col // grid_cols
    grid_col = col - grid_row * grid_cols
    tile = (grid_row // rows) * lon_n + grid_col // 128
    cell_row = lax.rem(grid_row, rows)
    cell_col = lax.rem(grid_col, 128)
    slot = (
        lax.broadcasted_iota(jnp.int32, col.shape, 0) * 128
        + lax.broadcasted_iota(jnp.int32, col.shape, 1)
    )
    tile = jnp.where(slot < count[0], tile, -1)
    tile_ref[...] = tile
    earlier = lax.broadcasted_iota(jnp.int32, (2 * WIDE, WIDE), 0)
    later = lax.broadcasted_iota(jnp.int32, (2 * WIDE, WIDE), 1)
    adder = jnp.where((earlier <= later) | (earlier >= WIDE), 1.0, 0.0).astype(BF16)
    ids = lax.broadcasted_iota(jnp.int32, (total, WIDE), 0)
    ranks = lax.broadcasted_iota(jnp.int32, (WIDE, WIDE), 0)
    seen = jnp.zeros((total, WIDE), F32)
    for c in range(pieces):
        hot = jnp.where(ids == tile[c : c + 1, :], 1.0, 0.0)
        both = jnp.concatenate([hot.astype(BF16), seen.astype(BF16)], axis=1)
        before = jnp.dot(both, adder, preferred_element_type=F32)
        rank = jnp.sum(hot * before, axis=0, keepdims=True).astype(jnp.int32) - 1
        rank_hot[:, c * WIDE : (c + 1) * WIDE] = jnp.where(ranks == rank, 1.0, 0.0).astype(BF16)
        seen = seen + hot

    kload.wait()
    for c in range(pieces):
        spot = pl.ds(c * WIDE, WIDE)
        pbuf[0:levels, spot] = kbuf[:, spot] * innov[c : c + 1, :]
        index = lax.broadcasted_iota(jnp.int32, (PAY - levels, WIDE), 0)
        pbuf[levels:PAY, spot] = jnp.where(
            index == 0,
            cell_row[c : c + 1, :].astype(F32),
            jnp.where(index == 1, cell_col[c : c + 1, :].astype(F32), 0.0),
        )

    pl.semaphore_wait(barrier, total - 1)

    def row_copy(field, g, side, start):
        at = pl.ds(g * GROUP, GROUP)
        if side == 0:
            src, dst, to = TOP + rows - 1, TOP - 1, (la + 1, lo)
        else:
            src, dst, to = TOP, TOP + rows, (la - 1, lo)
        k = 0 if field is q0 else 1
        return pltpu.make_async_remote_copy(
            src_ref=field.at[at, :, src, :],
            dst_ref=field.at[at, :, dst, :],
            send_sem=row_send.at[k, side, g],
            recv_sem=row_recv.at[k, side, g],
            device_id=to,
            device_id_type=MESH,
        )

    has_north = la < lat_n - 1
    has_south = la > 0

    def send_rows(field, g):
        @pl.when(has_north)
        def _():
            row_copy(field, g, 0, True).start()

        @pl.when(has_south)
        def _():
            row_copy(field, g, 1, True).start()

    def arrived_rows(field, g):
        @pl.when(has_south)
        def _():
            row_copy(field, g, 0, True).wait_recv()

        @pl.when(has_north)
        def _():
            row_copy(field, g, 1, True).wait_recv()

    def sent_rows(field, g):
        @pl.when(has_north)
        def _():
            row_copy(field, g, 0, True).wait_send()

        @pl.when(has_south)
        def _():
            row_copy(field, g, 1, True).wait_send()

    for field in (q0, q1):
        @pl.when(la == 0)
        def _():
            @pl.loop(0, tracers)
            def _(t):
                field[t, :, 0:TOP, :] = jnp.zeros((levels, TOP, 128), F32)

        @pl.when(la == lat_n - 1)
        def _():
            @pl.loop(0, tracers)
            def _(t):
                field[t, :, TOP + rows :, :] = jnp.zeros((levels, TOP, 128), F32)

    @pl.when(la == 0)
    def _():
        fq[:, 0:TOP, :] = jnp.zeros((levels, TOP, 128), F32)

    @pl.when(la == lat_n - 1)
    def _():
        fq[:, TOP + rows :, :] = jnp.zeros((levels, TOP, 128), F32)

    for g in range(chunks):
        loads[g].wait()
        send_rows(q0, g)

    def pay_copy(p, src):
        return pltpu.make_async_remote_copy(
            src_ref=send.at[p],
            dst_ref=recv.at[src],
            send_sem=pay_send.at[p],
            recv_sem=pay_recv.at[src],
            device_id=(p // lon_n, lax.rem(p, lon_n)),
            device_id_type=MESH,
        )

    own = pltpu.make_async_copy(send.at[me], recv.at[me], own_sem.at[0])

    @pl.loop(0, lat_n)
    def _(step):
        row = lax.rem(la + 1 + step, lat_n)

        for c in range(pieces):
            spot = pl.ds(c * WIDE, WIDE)
            block = pbuf[:, spot]
            hi = block.astype(BF16).astype(F32)
            low = block - hi
            where_to = jnp.broadcast_to(tile_ref[c : c + 1, :], (PAY, WIDE)) - row * lon_n
            for d in range(lon_n):
                mine = where_to == d
                a_hi[d * PAY : (d + 1) * PAY, spot] = jnp.where(mine, hi, 0.0).astype(BF16)
                a_lo[d * PAY : (d + 1) * PAY, spot] = jnp.where(mine, low, 0.0).astype(BF16)
        contract = (((1,), (1,)), ((), ()))
        packed = lax.dot_general(
            a_hi[...], rank_hot[...], contract, preferred_element_type=F32
        ) + lax.dot_general(a_lo[...], rank_hot[...], contract, preferred_element_type=F32)
        send[pl.ds(row * lon_n, lon_n)] = packed.reshape(lon_n, PAY, WIDE)

        @pl.loop(0, lon_n)
        def _(j):
            p = row * lon_n + j

            @pl.when(p != me)
            def _():
                pay_copy(p, me).start()

    own.start()

    lane = lax.broadcasted_iota(jnp.int32, (rows, 128), 1)
    first = lane == 0
    last = lane == 127

    def col_copy(k, g, side):
        return pltpu.make_async_remote_copy(
            src_ref=edge.at[k, g],
            dst_ref=(edge_w if side == 0 else edge_e).at[k, g],
            send_sem=col_send.at[k, side, g],
            recv_sem=col_recv.at[k, side, g],
            device_id=(la, east if side == 0 else west),
            device_id_type=MESH,
        )

    def gather_edges(read, count_blocks):
        lanes = lax.broadcasted_iota(jnp.int32, (BLOCK * rows, 128), 1)
        packed = jnp.zeros((BLOCK * rows, 128), F32)
        for k in range(count_blocks):
            block = read(k).reshape(BLOCK * rows, 128)
            packed = jnp.where(lanes // 2 == k, pltpu.roll(block, (1 + 2 * k) % 128, 1), packed)
        return packed.T

    def spread(from_e, from_w):
        tall = from_e.shape[0]
        odd = lax.rem(lax.broadcasted_iota(jnp.int32, (tall, 128), 0), 2) == 1
        mixed = jnp.where(odd, pltpu.roll(from_w, 1, 0), pltpu.roll(from_e, tall - 1, 0))
        if tall < 128:
            mixed = jnp.concatenate([mixed, jnp.zeros((128 - tall, 128), F32)], axis=0)
        return mixed.T

    def send_cols(field, k, g):
        def read(b):
            return field[
                g * GROUP + b // parts,
                pl.ds((b % parts) * BLOCK, BLOCK),
                pl.ds(TOP, rows),
                :,
            ]

        edge[k, g] = gather_edges(read, GROUP * parts)[: edge.shape[2]]
        for side in (0, 1):
            col_copy(k, g, side).start()

    @pl.loop(0, chunks)
    def _(g):
        send_cols(q0, 0, g)

    wload.wait()

    @pl.loop(0, levels)
    def _(l):
        u = wind[0, l]
        v = wind[1, l]
        coef[0, l] = 0.8 - jnp.abs(u) - jnp.abs(v) - 2.0 * vd[l]
        coef[1, l] = jnp.maximum(u, 0.0) + 0.05
        coef[2, l] = jnp.maximum(-u, 0.0) + 0.05
        coef[3, l] = jnp.maximum(v, 0.0) + 0.05
        coef[4, l] = jnp.maximum(-v, 0.0) + 0.05

    def stencil(read, l, edges, k, cs):
        q = read(l, TOP)
        beside = pltpu.roll(edges, 127 - 2 * k, 1)
        e = jnp.where(last, beside, pltpu.roll(q, 127, 1))
        w = jnp.where(first, beside, pltpu.roll(q, 1, 1))
        n = read(l, TOP + 1)
        s = read(l, TOP - 1)
        up = read(jnp.minimum(l + 1, levels - 1), TOP)
        down = read(jnp.maximum(l - 1, 0), TOP)
        c0, ce, cw, cn, cs_, cv = cs
        return (c0 * q + ce * e) + (cw * w + cn * n) + (cs_ * s + cv * (up + down))

    def coefs(l):
        return tuple(coef[i, l] for i in range(5)) + (vd[l],)

    def advance(field, k, g, write):
        arrived_rows(field, g)
        for side in (0, 1):
            col_copy(k, g, side).wait_recv()
        halo[...] = spread(edge_e[k, g], edge_w[k, g])
        for part in range(parts):
            @pl.loop(0, BLOCK)
            def _(j):
                l = part * BLOCK + j
                cs = coefs(l)
                edges = halo[pl.ds(pl.multiple_of(j * rows, rows), rows), :]
                for i in range(GROUP):
                    t = g * GROUP + i

                    def read(level, r):
                        return field[t, level, pl.ds(r, rows), :]

                    write(i, t, l, stencil(read, l, edges, i * parts + part, cs))

    @pl.loop(0, chunks)
    def _(g):
        def write(i, t, l, value):
            q1[t, l, TOP : TOP + rows, :] = value

        advance(q0, 0, g, write)
        send_rows(q1, g)
        send_cols(q1, 1, g)

    def out_copy(g):
        at = pl.ds(g * GROUP, GROUP)
        return pltpu.make_async_copy(obuf.at[at], out.at[at], out_sem.at[g])

    @pl.loop(0, chunks)
    def _(g):
        def write(i, t, l, value):
            obuf[t, l] = value

        advance(q1, 1, g, write)
        out_copy(g).start()

    own.wait()
    tile_rows = lax.broadcasted_iota(jnp.int32, (rows, WIDE), 0)
    fq[:, TOP : TOP + rows, :] = jnp.zeros((levels, rows, 128), F32)

    @pl.loop(0, lat_n)
    def _(step):
        source_row = lax.rem(la + lat_n - 1 - step + lat_n, lat_n)

        @pl.loop(0, lon_n)
        def _(j):
            src = source_row * lon_n + j

            @pl.when(src != me)
            def _():
                pay_copy(src, src).wait_recv()

        columns = []
        for j in range(lon_n):
            block = recv[source_row * lon_n + j]
            hi = block.astype(BF16).astype(F32)
            low = block - hi
            here = tile_rows == block[levels : levels + 1, :].astype(jnp.int32)
            spot = pl.ds(j * WIDE, WIDE)
            for l in range(levels):
                b_hi[l * rows : (l + 1) * rows, spot] = jnp.where(
                    here, hi[l : l + 1, :], 0.0
                ).astype(BF16)
                b_lo[l * rows : (l + 1) * rows, spot] = jnp.where(
                    here, low[l : l + 1, :], 0.0
                ).astype(BF16)
            columns.append(
                jnp.where(
                    ranks == block[levels + 1 : levels + 2, :].astype(jnp.int32), 1.0, 0.0
                ).astype(BF16)
            )
        hot = jnp.concatenate(columns, axis=1)
        contract = (((1,), (1,)), ((), ()))
        part = lax.dot_general(
            b_hi[...], hot, contract, preferred_element_type=F32
        ) + lax.dot_general(b_lo[...], hot, contract, preferred_element_type=F32)
        fq[:, TOP : TOP + rows, :] += part.reshape(levels, rows, 128)

    def f_rows(side):
        if side == 0:
            src, dst, to = TOP + rows - 1, TOP - 1, (la + 1, lo)
        else:
            src, dst, to = TOP, TOP + rows, (la - 1, lo)
        return pltpu.make_async_remote_copy(
            src_ref=fq.at[:, src, :],
            dst_ref=fq.at[:, dst, :],
            send_sem=f_send.at[side],
            recv_sem=f_recv.at[side],
            device_id=to,
            device_id_type=MESH,
        )

    def f_cols(side):
        return pltpu.make_async_remote_copy(
            src_ref=fedge,
            dst_ref=fedge_w if side == 0 else fedge_e,
            send_sem=f_send.at[2 + side],
            recv_sem=f_recv.at[2 + side],
            device_id=(la, east if side == 0 else west),
            device_id_type=MESH,
        )

    @pl.when(has_north)
    def _():
        f_rows(0).start()

    @pl.when(has_south)
    def _():
        f_rows(1).start()

    fedge[...] = gather_edges(
        lambda b: fq[pl.ds(b * BLOCK, BLOCK), pl.ds(TOP, rows), :], parts
    )[: fedge.shape[0]]
    for side in (0, 1):
        f_cols(side).start()
    for side in (0, 1):
        f_cols(side).wait_recv()

    @pl.when(has_south)
    def _():
        f_rows(0).wait_recv()

    @pl.when(has_north)
    def _():
        f_rows(1).wait_recv()

    halo[...] = spread(fedge_e[...], fedge_w[...])
    for part in range(parts):
        @pl.loop(0, BLOCK)
        def _(j):
            l = part * BLOCK + j

            def read(level, r):
                return fq[level, pl.ds(r, rows), :]

            edges = halo[pl.ds(pl.multiple_of(j * rows, rows), rows), :]
            sf[l] = stencil(read, l, edges, part, coefs(l))

    @pl.loop(0, total)
    def _(p):
        @pl.when(p != me)
        def _():
            pay_copy(p, me).wait_send()

    @pl.loop(0, chunks)
    def _(g):
        for k, field in ((0, q0), (1, q1)):
            sent_rows(field, g)
            for side in (0, 1):
                col_copy(k, g, side).wait_send()
        out_copy(g).wait()

    @pl.when(has_north)
    def _():
        f_rows(0).wait_send()

    @pl.when(has_south)
    def _():
        f_rows(1).wait_send()

    for side in (0, 1):
        f_cols(side).wait_send()


def per_device(adjoint, courant, vert_diff, kernel, innovation, sound_col, sound_count):
    tracers, levels, rows, columns = adjoint.shape
    lat_n = lax.axis_size("lat")
    lon_n = lax.axis_size("lon")
    total = lat_n * lon_n
    slots = sound_col.shape[0]
    chunks = tracers // GROUP
    parts = levels // BLOCK
    assert columns == 128 and rows == 16 and 2 * slots // total <= WIDE
    tall = rows + 2 * TOP
    edge_rows = -(-2 * GROUP * parts // 8) * 8
    vmem = pl.BlockSpec(memory_space=pltpu.VMEM)
    smem = pl.BlockSpec(memory_space=pltpu.SMEM)
    hbm = pl.BlockSpec(memory_space=pl.ANY)
    dma = pltpu.SemaphoreType.DMA
    twice, forced = pl.pallas_call(
        functools.partial(kernel_body, lat_n, lon_n, tracers, levels, rows),
        out_shape=(
            jax.ShapeDtypeStruct(adjoint.shape, F32),
            jax.ShapeDtypeStruct((levels, rows, 128), F32),
        ),
        in_specs=[hbm, hbm, hbm, smem, smem, vmem, vmem],
        out_specs=(hbm, vmem),
        scratch_shapes=[
            pltpu.VMEM((tracers, levels, tall, 128), F32),
            pltpu.VMEM((tracers, levels, tall, 128), F32),
            pltpu.VMEM((levels, tall, 128), F32),
            pltpu.VMEM((2, levels, rows, 128), F32),
            pltpu.VMEM((5, levels, rows, 128), F32),
            pltpu.VMEM((levels, slots), F32),
            pltpu.VMEM((PAY, slots), F32),
            pltpu.VMEM((total, PAY, WIDE), F32),
            pltpu.VMEM((total, PAY, WIDE), F32),
            pltpu.VMEM((lon_n * PAY, slots), BF16),
            pltpu.VMEM((lon_n * PAY, slots), BF16),
            pltpu.VMEM((levels * rows, lon_n * WIDE), BF16),
            pltpu.VMEM((levels * rows, lon_n * WIDE), BF16),
            pltpu.VMEM((WIDE, slots), BF16),
            pltpu.VMEM((slots // 128, 128), jnp.int32),
            pltpu.VMEM((2, chunks, edge_rows, 128), F32),
            pltpu.VMEM((2, chunks, edge_rows, 128), F32),
            pltpu.VMEM((2, chunks, edge_rows, 128), F32),
            pltpu.VMEM((BLOCK * rows, 128), F32),
            pltpu.VMEM((8, 128), F32),
            pltpu.VMEM((8, 128), F32),
            pltpu.VMEM((8, 128), F32),
            pltpu.VMEM(adjoint.shape, F32),
            dma((2 + chunks,)),
            dma((2, 2, chunks)),
            dma((2, 2, chunks)),
            dma((2, 2, chunks)),
            dma((2, 2, chunks)),
            dma((total,)),
            dma((total,)),
            dma((4,)),
            dma((4,)),
            dma((chunks,)),
            dma((1,)),
        ],
        compiler_params=pltpu.CompilerParams(
            collective_id=0, has_side_effects=True, vmem_limit_bytes=48 * 1024 * 1024
        ),
    )(
        adjoint,
        courant,
        kernel,
        vert_diff,
        sound_count,
        innovation.reshape(slots // 128, 128),
        sound_col.reshape(slots // 128, 128),
    )
    return twice + forced[None]


def solution(mesh):
    placed = (
        P(None, None, "lat", "lon"),
        P(None, None, "lat", "lon"),
        P(),
        P(None, ("lat", "lon")),
        P(("lat", "lon")),
        P(("lat", "lon")),
        P(("lat", "lon")),
    )
    return jax.shard_map(
        per_device,
        mesh=mesh,
        in_specs=placed,
        out_specs=P(None, None, "lat", "lon"),
        check_vma=False,
    )
```

time: 223 us -> 58.5 us (0.26)
  local copies, waits for them, and re-layouts: 101 us -> 3.96 us
  other arithmetic: 82.5 us -> 1.88 us
  Pallas kernels: 0 us -> 51.7 us
  starting transfers between devices: 24.4 us -> 0 us
  waiting for transfers between devices: 12.5 us -> 0 us
    pallas_call x0 -> x1, Pallas kernels: none -> 51.7 us  [per_device(): pl.pallas_call(functools.partial(kernel_body, lat_n, lon_n, tracers, leve...]
    scatter-add x1 -> x0, other arithmetic: 22.7 us -> none  [per_device(): jnp.zeros((levels, ncell), jnp.float32).at[:, index]]
    unnamed x29 -> x10, local copies, waits for them, and re-layouts: 24.1 us -> 3.96 us
    slice x9 -> x0, local copies, waits for them, and re-layouts: 18.7 us -> none  [the longest x4 10.1 us: advance(): lower = jnp.concatenate([centre[:, :1], centre[:, :-1]], axis=1)]
    ppermute x6 -> x0, local copies, waits for them, and re-layouts: 17.4 us -> none  [the longest x3 9.3 us: padded_2(): lax.ppermute(tail, axis, [(i, (i + 1) % count) for i in range(count)])]
    add x2 -> x1, other arithmetic: 18.4 us -> 1.88 us  [per_device(): return twice + forced[None]]
    another operation x3 -> x0, other arithmetic: 16.2 us -> none
    mul x4 -> x0, other arithmetic: 15.3 us -> none  [the longest x2 11.8 us: single_step(): padded_2(field, (('lat', 2), ('lon', 3)), 1) * row_mask(rows_tile, 1)]
  transfers between devices with their start and end apart: 10 -> 0, of which waited for: 3 -> 0; matrix products, arithmetic and copies ran while one was open for 47% -> 0% of each run, Pallas kernels for 0% -> 0%
where the time goes in v1:
time: 58.5 us; the launch traced here: 58.2 us
  Pallas kernels  51.7 us (88%)
  local copies, waits for them, and re-layouts  3.96 us (7%)
  other arithmetic  1.88 us (3%)
  between operations  0.67 us (1%)
    pallas_call x1, Pallas kernels, per_device(): pl.pallas_call(functools.partial(kernel_body, lat_n, lon_n, tracers, leve...  51.7 us
    unnamed x10, local copies, waits for them, and re-layouts  3.96 us
    add x1, other arithmetic, per_device(): return twice + forced[None]  1.88 us

profile of v1, /device:TPU:0, one launch (start us, length us, event | category | flops | bytes accessed | tf_op | source)
XLA Modules:
  0.0 58.2 jit_solution(7312730105136285559)
XLA Ops:
  0.7 0.0 copy-start
  0.7 1.0 %copy-done = f32[2,24,16,128]{3,2,1,0:T(8,128)S(1)} copy-done((f32[2,24,16,128]{3,2,1,0:T(8,128)S(1)}, f32[2,24,16,128]{3,2,1,0:T(8,128)}, u32[]{:S(2)}) %copy-start) | copy-done | bytes 393240
  1.6 0.0 copy-start.1
  1.7 0.9 %copy-done.1 = f32[24,2048]{1,0:T(8,128)S(1)} copy-done((f32[24,2048]{1,0:T(8,128)S(1)}, f32[24,2048]{1,0:T(8,128)}, u32[]{:S(2)}) %copy-start.1) | copy-done | bytes 196632
  2.6 0.0 copy-start.2
  2.6 0.7 %copy-done.2 = f32[2048]{0:T(1024)S(1)} copy-done((f32[2048]{0:T(1024)S(1)}, f32[2048]{0:T(1024)}, u32[]{:S(2)}) %copy-start.2) | copy-done | bytes 8216
  3.3 0.0 copy-start.3
  3.3 0.7 %copy-done.3 = s32[2048]{0:T(1024)S(1)} copy-done((s32[2048]{0:T(1024)S(1)}, s32[2048]{0:T(1024)}, u32[]{:S(2)}) %copy-start.3) | copy-done | bytes 8216
  4.0 0.0 copy-start.4
  4.0 0.7 %copy-done.4 = f32[24]{0:T(128)S(1)} copy-done((f32[24]{0:T(128)S(1)}, f32[24]{0:T(128)}, u32[]{:S(2)}) %copy-start.4) | copy-done | bytes 120
  4.6 51.7 %shard_map.73 = (f32[16,24,16,128]{3,2,1,0:T(8,128)S(1)}, f32[24,16,128]{2,1,0:T(8,128)S(1)}) custom-call(f32[16,24,16,128]{3,2,1,0:T(8,128)} %adj.1, f32[2,24,16,128]{3,2,1,0:T(8,128)S(1)} %copy-done, f32[24,2048]{1,0:T(8,128)S(1)} %copy-done.1, f32[24]{0:T(128)S(1)} %copy-done.4, s32[1]{0:T(128)S(6)} %copy.8.count, f32[16,128]{1,0:T(8,128)S(1)} %bitcast.2, ...), custom_call_target="tpu_custom_call" | custom-call | tf_op jit(solution)/shard_map/pallas_call | solution.py:474
  56.3 1.9 %broadcast_add_fusion = f32[16,24,16,128]{3,2,1,0:T(8,128)} fusion(f32[16,24,16,128]{3,2,1,0:T(8,128)S(1)} %get-tuple-element.7, f32[24,16,128]{2,1,0:T(8,128)S(1)} %get-tuple-element.8), kind=kLoop, calls=%fused_computation | loop fusion | flops 786432 | bytes 6488064 | tf_op jit(solution)/shard_map/add | solution.py:530
Async XLA Ops:
  0.7 1.0 %copy-start = (f32[2,24,16,128]{3,2,1,0:T(8,128)S(1)}, f32[2,24,16,128]{3,2,1,0:T(8,128)}, u32[]{:S(2)}) copy-start(f32[2,24,16,128]{3,2,1,0:T(8,128)} %cour.1) | copy-start | bytes 1179652
  1.6 0.9 %copy-start.1 = (f32[24,2048]{1,0:T(8,128)S(1)}, f32[24,2048]{1,0:T(8,128)}, u32[]{:S(2)}) copy-start(f32[24,2048]{1,0:T(8,128)} %kern.1) | copy-start | bytes 589828
  2.6 0.7 %copy-start.2 = (f32[2048]{0:T(1024)S(1)}, f32[2048]{0:T(1024)}, u32[]{:S(2)}) copy-start(f32[2048]{0:T(1024)} %param.11) | copy-start | bytes 24580
  3.3 0.7 %copy-start.3 = (s32[2048]{0:T(1024)S(1)}, s32[2048]{0:T(1024)}, u32[]{:S(2)}) copy-start(s32[2048]{0:T(1024)} %param.12) | copy-start | bytes 24580
  4.0 0.7 %copy-start.4 = (f32[24]{0:T(128)S(1)}, f32[24]{0:T(128)}, u32[]{:S(2)}) copy-start(f32[24]{0:T(128)} %vd.1) | copy-start | bytes 292

commit v2 on v1

--- a/solution.py
+++ b/solution.py
@@ -19,10 +19,10 @@
 
 def kernel_body(
     lat_n, lon_n, tracers, levels, rows,
-    adj, cour, kern, vd, count, innov, cols,
+    adj, cour, kern, vd, count, innov_hbm, cols_hbm,
     out, sf,
     q0, q1, fq, wind, coef, kbuf, pbuf, send, recv, a_hi, a_lo, b_hi, b_lo,
-    rank_hot, tile_ref, edge, edge_e, edge_w, halo, fedge, fedge_e, fedge_w, obuf,
+    rank_hot, tile_ref, edge, edge_e, edge_w, halo, fedge, fedge_e, fedge_w, innov, cols, obuf,
     load_sem, row_send, row_recv, col_send, col_recv, pay_send, pay_recv,
     f_send, f_recv, out_sem, own_sem,
 ):
@@ -46,6 +46,10 @@
             barrier, inc=1, device_id=(p // lon_n, lax.rem(p, lon_n)), device_id_type=MESH
         )
 
+    cload = pltpu.make_async_copy(cols_hbm, cols, load_sem.at[2])
+    cload.start()
+    iload = pltpu.make_async_copy(innov_hbm, innov, load_sem.at[3])
+    iload.start()
     kload = pltpu.make_async_copy(kern, kbuf, load_sem.at[0])
     kload.start()
     loads = []
@@ -54,13 +58,14 @@
             pltpu.make_async_copy(
                 adj.at[pl.ds(g * GROUP, GROUP)],
                 q0.at[pl.ds(g * GROUP, GROUP), :, pl.ds(TOP, rows), :],
-                load_sem.at[2 + g],
+                load_sem.at[4 + g],
             )
         )
         loads[-1].start()
     wload = pltpu.make_async_copy(cour, wind, load_sem.at[1])
     wload.start()
 
+    cload.wait()
     col = cols[...]
     grid_cols = lon_n * 128
     grid_row = col // grid_cols
@@ -89,6 +94,7 @@
         seen = seen + hot
 
     kload.wait()
+    iload.wait()
     for c in range(pieces):
         spot = pl.ds(c * WIDE, WIDE)
         pbuf[0:levels, spot] = kbuf[:, spot] * innov[c : c + 1, :]
@@ -171,6 +177,53 @@
     for g in range(chunks):
         loads[g].wait()
         send_rows(q0, g)
+
+    lane = lax.broadcasted_iota(jnp.int32, (rows, 128), 1)
+    first = lane == 0
+    last = lane == 127
+
+    def col_copy(k, g, side):
+        return pltpu.make_async_remote_copy(
+            src_ref=edge.at[k, g],
+            dst_ref=(edge_w if side == 0 else edge_e).at[k, g],
+            send_sem=col_send.at[k, side, g],
+            recv_sem=col_recv.at[k, side, g],
+            device_id=(la, east if side == 0 else west),
+            device_id_type=MESH,
+        )
+
+    def gather_edges(read, count_blocks):
+        lanes = lax.broadcasted_iota(jnp.int32, (BLOCK * rows, 128), 1)
+        packed = jnp.zeros((BLOCK * rows, 128), F32)
+        for k in range(count_blocks):
+            block = read(k).reshape(BLOCK * rows, 128)
+            packed = jnp.where(lanes // 2 == k, pltpu.roll(block, (1 + 2 * k) % 128, 1), packed)
+        return packed.T
+
+    def spread(from_e, from_w):
+        tall = from_e.shape[0]
+        odd = lax.rem(lax.broadcasted_iota(jnp.int32, (tall, 128), 0), 2) == 1
+        mixed = jnp.where(odd, pltpu.roll(from_w, 1, 0), pltpu.roll(from_e, tall - 1, 0))
+        if tall < 128:
+            mixed = jnp.concatenate([mixed, jnp.zeros((128 - tall, 128), F32)], axis=0)
+        return mixed.T
+
+    def send_cols(field, k, g):
+        def read(b):
+            return field[
+                g * GROUP + b // parts,
+                pl.ds((b % parts) * BLOCK, BLOCK),
+                pl.ds(TOP, rows),
+                :,
+            ]
+
+        edge[k, g] = gather_edges(read, GROUP * parts)[: edge.shape[2]]
+        for side in (0, 1):
+            col_copy(k, g, side).start()
+
+    @pl.loop(0, chunks)
+    def _(g):
+        send_cols(q0, 0, g)
 
     def pay_copy(p, src):
         return pltpu.make_async_remote_copy(
@@ -214,56 +267,9 @@
 
     own.start()
 
-    lane = lax.broadcasted_iota(jnp.int32, (rows, 128), 1)
-    first = lane == 0
-    last = lane == 127
-
-    def col_copy(k, g, side):
-        return pltpu.make_async_remote_copy(
-            src_ref=edge.at[k, g],
-            dst_ref=(edge_w if side == 0 else edge_e).at[k, g],
-            send_sem=col_send.at[k, side, g],
-            recv_sem=col_recv.at[k, side, g],
-            device_id=(la, east if side == 0 else west),
-            device_id_type=MESH,
-        )
-
-    def gather_edges(read, count_blocks):
-        lanes = lax.broadcasted_iota(jnp.int32, (BLOCK * rows, 128), 1)
-        packed = jnp.zeros((BLOCK * rows, 128), F32)
-        for k in range(count_blocks):
-            block = read(k).reshape(BLOCK * rows, 128)
-            packed = jnp.where(lanes // 2 == k, pltpu.roll(block, (1 + 2 * k) % 128, 1), packed)
-        return packed.T
-
-    def spread(from_e, from_w):
-        tall = from_e.shape[0]
-        odd = lax.rem(lax.broadcasted_iota(jnp.int32, (tall, 128), 0), 2) == 1
-        mixed = jnp.where(odd, pltpu.roll(from_w, 1, 0), pltpu.roll(from_e, tall - 1, 0))
-        if tall < 128:
-            mixed = jnp.concatenate([mixed, jnp.zeros((128 - tall, 128), F32)], axis=0)
-        return mixed.T
-
-    def send_cols(field, k, g):
-        def read(b):
-            return field[
-                g * GROUP + b // parts,
-                pl.ds((b % parts) * BLOCK, BLOCK),
-                pl.ds(TOP, rows),
-                :,
-            ]
-
-        edge[k, g] = gather_edges(read, GROUP * parts)[: edge.shape[2]]
-        for side in (0, 1):
-            col_copy(k, g, side).start()
-
-    @pl.loop(0, chunks)
-    def _(g):
-        send_cols(q0, 0, g)
-
     wload.wait()
 
-    @pl.loop(0, levels)
+    @pl.loop(0, levels, unroll=4)
     def _(l):
         u = wind[0, l]
         v = wind[1, l]
@@ -280,8 +286,8 @@
         w = jnp.where(first, beside, pltpu.roll(q, 1, 1))
         n = read(l, TOP + 1)
         s = read(l, TOP - 1)
-        up = read(jnp.minimum(l + 1, levels - 1), TOP)
-        down = read(jnp.maximum(l - 1, 0), TOP)
+        up = read(min(l + 1, levels - 1) if isinstance(l, int) else jnp.minimum(l + 1, levels - 1), TOP)
+        down = read(max(l - 1, 0) if isinstance(l, int) else jnp.maximum(l - 1, 0), TOP)
         c0, ce, cw, cn, cs_, cv = cs
         return (c0 * q + ce * e) + (cw * w + cn * n) + (cs_ * s + cv * (up + down))
 
@@ -294,18 +300,23 @@
             col_copy(k, g, side).wait_recv()
         halo[...] = spread(edge_e[k, g], edge_w[k, g])
         for part in range(parts):
-            @pl.loop(0, BLOCK)
-            def _(j):
-                l = part * BLOCK + j
-                cs = coefs(l)
-                edges = halo[pl.ds(pl.multiple_of(j * rows, rows), rows), :]
-                for i in range(GROUP):
-                    t = g * GROUP + i
-
-                    def read(level, r):
-                        return field[t, level, pl.ds(r, rows), :]
-
-                    write(i, t, l, stencil(read, l, edges, i * parts + part, cs))
+            @pl.loop(0, BLOCK // 4)
+            def _(pair):
+                done = []
+                for near in range(4):
+                    j = pair * 4 + near
+                    l = part * BLOCK + j
+                    cs = coefs(l)
+                    edges = halo[pl.ds(pl.multiple_of(j * rows, rows), rows), :]
+                    for i in range(GROUP):
+                        t = g * GROUP + i
+
+                        def read(level, r):
+                            return field[t, level, pl.ds(r, rows), :]
+
+                        done.append((i, t, l, stencil(read, l, edges, i * parts + part, cs)))
+                for item in done:
+                    write(*item)
 
     @pl.loop(0, chunks)
     def _(g):
@@ -420,15 +431,17 @@
 
     halo[...] = spread(fedge_e[...], fedge_w[...])
     for part in range(parts):
-        @pl.loop(0, BLOCK)
-        def _(j):
+        done = []
+        for j in range(BLOCK):
             l = part * BLOCK + j
 
             def read(level, r):
                 return fq[level, pl.ds(r, rows), :]
 
-            edges = halo[pl.ds(pl.multiple_of(j * rows, rows), rows), :]
-            sf[l] = stencil(read, l, edges, part, coefs(l))
+            edges = halo[j * rows : (j + 1) * rows, :]
+            done.append((l, stencil(read, l, edges, part, coefs(l))))
+        for l, value in done:
+            sf[l] = value
 
     @pl.loop(0, total)
     def _(p):
@@ -469,7 +482,7 @@
     edge_rows = -(-2 * GROUP * parts // 8) * 8
     vmem = pl.BlockSpec(memory_space=pltpu.VMEM)
     smem = pl.BlockSpec(memory_space=pltpu.SMEM)
-    hbm = pl.BlockSpec(memory_space=pl.ANY)
+    far = pl.BlockSpec(memory_space=pltpu.HBM)
     dma = pltpu.SemaphoreType.DMA
     twice, forced = pl.pallas_call(
         functools.partial(kernel_body, lat_n, lon_n, tracers, levels, rows),
@@ -477,8 +490,8 @@
             jax.ShapeDtypeStruct(adjoint.shape, F32),
             jax.ShapeDtypeStruct((levels, rows, 128), F32),
         ),
-        in_specs=[hbm, hbm, hbm, smem, smem, vmem, vmem],
-        out_specs=(hbm, vmem),
+        in_specs=[far, far, far, smem, smem, far, far],
+        out_specs=(far, vmem),
         scratch_shapes=[
             pltpu.VMEM((tracers, levels, tall, 128), F32),
             pltpu.VMEM((tracers, levels, tall, 128), F32),
@@ -502,8 +515,10 @@
             pltpu.VMEM((8, 128), F32),
             pltpu.VMEM((8, 128), F32),
             pltpu.VMEM((8, 128), F32),
+            pltpu.VMEM((slots // 128, 128), F32),
+            pltpu.VMEM((slots // 128, 128), jnp.int32),
             pltpu.VMEM(adjoint.shape, F32),
-            dma((2 + chunks,)),
+            dma((4 + chunks,)),
             dma((2, 2, chunks)),
             dma((2, 2, chunks)),
             dma((2, 2, chunks)),
@@ -516,7 +531,7 @@
             dma((1,)),
         ],
         compiler_params=pltpu.CompilerParams(
-            collective_id=0, has_side_effects=True, vmem_limit_bytes=48 * 1024 * 1024
+            collective_id=0, has_side_effects=True, vmem_limit_bytes=62 * 1024 * 1024
         ),
     )(
         adjoint,

time: 58.5 us -> 46.9 us (0.80)
  Pallas kernels: 51.7 us -> 42.3 us
  local copies, waits for them, and re-layouts: 3.96 us -> 0 us
  other arithmetic: 1.88 us -> 3.81 us
    pallas_call x1, Pallas kernels: 51.7 us -> 42.3 us  [per_device(): pl.pallas_call(functools.partial(kernel_body, lat_n, lon_n, tracers, leve...]
    unnamed x10 -> x0, local copies, waits for them, and re-layouts: 3.96 us -> none
    add x1, other arithmetic: 1.88 us -> 3.81 us  [per_device(): return twice + forced[None]]
where the time goes in v2:
time: 46.9 us; the launch traced here: 46.7 us
  Pallas kernels  42.3 us (90%)
  other arithmetic  3.81 us (8%)
  between operations  0.66 us (1%)
    pallas_call x1, Pallas kernels, per_device(): pl.pallas_call(functools.partial(kernel_body, lat_n, lon_n, tracers, leve...  42.3 us
    add x1, other arithmetic, per_device(): return twice + forced[None]  3.81 us

profile of v2, /device:TPU:0, one launch (start us, length us, event | category | flops | bytes accessed | tf_op | source)
XLA Modules:
  0.0 46.7 jit_solution(14841014389529683134)
XLA Ops:
  0.7 42.3 %shard_map.73 = (f32[16,24,16,128]{3,2,1,0:T(8,128)}, f32[24,16,128]{2,1,0:T(8,128)}) custom-call(f32[16,24,16,128]{3,2,1,0:T(8,128)} %adj.1, f32[2,24,16,128]{3,2,1,0:T(8,128)} %cour.1, f32[24,2048]{1,0:T(8,128)} %kern.1, f32[24]{0:T(128)} %vd.1, s32[1]{0:T(128)S(6)} %copy.8.count, f32[16,128]{1,0:T(8,128)} %bitcast.2, s32[16,128]{1,0:T(8,128)} %bitcast.3), custom_call_target="tpu_custom_call" | custom-call | tf_op jit(solution)/shard_map/pallas_call | solution.py:487
  42.9 3.8 %broadcast_add_fusion = f32[16,24,16,128]{3,2,1,0:T(8,128)} fusion(f32[16,24,16,128]{3,2,1,0:T(8,128)} %get-tuple-element.7, f32[24,16,128]{2,1,0:T(8,128)} %get-tuple-element.8), kind=kLoop, calls=%fused_computation | loop fusion | flops 786432 | bytes 6488064 | tf_op jit(solution)/shard_map/add | solution.py:545

commit v3 on v2

--- a/solution.py
+++ b/solution.py
@@ -227,8 +227,8 @@
 
     def pay_copy(p, src):
         return pltpu.make_async_remote_copy(
-            src_ref=send.at[p],
-            dst_ref=recv.at[src],
+            src_ref=send.at[p, pl.ds(0, levels + 2)],
+            dst_ref=recv.at[src, pl.ds(0, levels + 2)],
             send_sem=pay_send.at[p],
             recv_sem=pay_recv.at[src],
             device_id=(p // lon_n, lax.rem(p, lon_n)),
@@ -259,7 +259,7 @@
 
         @pl.loop(0, lon_n)
         def _(j):
-            p = row * lon_n + j
+            p = row * lon_n + lax.rem(lo + 1 + j, lon_n)
 
             @pl.when(p != me)
             def _():
@@ -300,11 +300,11 @@
             col_copy(k, g, side).wait_recv()
         halo[...] = spread(edge_e[k, g], edge_w[k, g])
         for part in range(parts):
-            @pl.loop(0, BLOCK // 4)
+            @pl.loop(0, BLOCK // 8)
             def _(pair):
                 done = []
-                for near in range(4):
-                    j = pair * 4 + near
+                for near in range(8):
+                    j = pair * 8 + near
                     l = part * BLOCK + j
                     cs = coefs(l)
                     edges = halo[pl.ds(pl.multiple_of(j * rows, rows), rows), :]

time: 46.9 us -> 45.1 us (0.962)
  Pallas kernels: 42.3 us -> 40.5 us
    pallas_call x1, Pallas kernels: 42.3 us -> 40.5 us  [per_device(): pl.pallas_call(functools.partial(kernel_body, lat_n, lon_n, tracers, leve...]
where the time goes in v3:
time: 45.1 us; the launch traced here: 44.9 us
  Pallas kernels  40.5 us (90%)
  other arithmetic  3.81 us (8%)
  between operations  0.66 us (1%)
    pallas_call x1, Pallas kernels, per_device(): pl.pallas_call(functools.partial(kernel_body, lat_n, lon_n, tracers, leve...  40.5 us
    add x1, other arithmetic, per_device(): return twice + forced[None]  3.81 us

profile of v3, /device:TPU:0, one launch (start us, length us, event | category | flops | bytes accessed | tf_op | source)
XLA Modules:
  0.0 44.9 jit_solution(7644995092482881212)
XLA Ops:
  0.7 40.5 %shard_map.73 = (f32[16,24,16,128]{3,2,1,0:T(8,128)}, f32[24,16,128]{2,1,0:T(8,128)}) custom-call(f32[16,24,16,128]{3,2,1,0:T(8,128)} %adj.1, f32[2,24,16,128]{3,2,1,0:T(8,128)} %cour.1, f32[24,2048]{1,0:T(8,128)} %kern.1, f32[24]{0:T(128)} %vd.1, s32[1]{0:T(128)S(6)} %copy.8.count, f32[16,128]{1,0:T(8,128)} %bitcast.2, s32[16,128]{1,0:T(8,128)} %bitcast.3), custom_call_target="tpu_custom_call" | custom-call | tf_op jit(solution)/shard_map/pallas_call | solution.py:487
  41.1 3.8 %broadcast_add_fusion = f32[16,24,16,128]{3,2,1,0:T(8,128)} fusion(f32[16,24,16,128]{3,2,1,0:T(8,128)} %get-tuple-element.7, f32[24,16,128]{2,1,0:T(8,128)} %get-tuple-element.8), kind=kLoop, calls=%fused_computation | loop fusion | flops 786432 | bytes 6488064 | tf_op jit(solution)/shard_map/add | solution.py:545

commit v4 on v3

--- a/solution.py
+++ b/solution.py
@@ -174,57 +174,6 @@
     def _():
         fq[:, TOP + rows :, :] = jnp.zeros((levels, TOP, 128), F32)
 
-    for g in range(chunks):
-        loads[g].wait()
-        send_rows(q0, g)
-
-    lane = lax.broadcasted_iota(jnp.int32, (rows, 128), 1)
-    first = lane == 0
-    last = lane == 127
-
-    def col_copy(k, g, side):
-        return pltpu.make_async_remote_copy(
-            src_ref=edge.at[k, g],
-            dst_ref=(edge_w if side == 0 else edge_e).at[k, g],
-            send_sem=col_send.at[k, side, g],
-            recv_sem=col_recv.at[k, side, g],
-            device_id=(la, east if side == 0 else west),
-            device_id_type=MESH,
-        )
-
-    def gather_edges(read, count_blocks):
-        lanes = lax.broadcasted_iota(jnp.int32, (BLOCK * rows, 128), 1)
-        packed = jnp.zeros((BLOCK * rows, 128), F32)
-        for k in range(count_blocks):
-            block = read(k).reshape(BLOCK * rows, 128)
-            packed = jnp.where(lanes // 2 == k, pltpu.roll(block, (1 + 2 * k) % 128, 1), packed)
-        return packed.T
-
-    def spread(from_e, from_w):
-        tall = from_e.shape[0]
-        odd = lax.rem(lax.broadcasted_iota(jnp.int32, (tall, 128), 0), 2) == 1
-        mixed = jnp.where(odd, pltpu.roll(from_w, 1, 0), pltpu.roll(from_e, tall - 1, 0))
-        if tall < 128:
-            mixed = jnp.concatenate([mixed, jnp.zeros((128 - tall, 128), F32)], axis=0)
-        return mixed.T
-
-    def send_cols(field, k, g):
-        def read(b):
-            return field[
-                g * GROUP + b // parts,
-                pl.ds((b % parts) * BLOCK, BLOCK),
-                pl.ds(TOP, rows),
-                :,
-            ]
-
-        edge[k, g] = gather_edges(read, GROUP * parts)[: edge.shape[2]]
-        for side in (0, 1):
-            col_copy(k, g, side).start()
-
-    @pl.loop(0, chunks)
-    def _(g):
-        send_cols(q0, 0, g)
-
     def pay_copy(p, src):
         return pltpu.make_async_remote_copy(
             src_ref=send.at[p, pl.ds(0, levels + 2)],
@@ -266,6 +215,57 @@
                 pay_copy(p, me).start()
 
     own.start()
+
+    for g in range(chunks):
+        loads[g].wait()
+        send_rows(q0, g)
+
+    lane = lax.broadcasted_iota(jnp.int32, (rows, 128), 1)
+    first = lane == 0
+    last = lane == 127
+
+    def col_copy(k, g, side):
+        return pltpu.make_async_remote_copy(
+            src_ref=edge.at[k, g],
+            dst_ref=(edge_w if side == 0 else edge_e).at[k, g],
+            send_sem=col_send.at[k, side, g],
+            recv_sem=col_recv.at[k, side, g],
+            device_id=(la, east if side == 0 else west),
+            device_id_type=MESH,
+        )
+
+    def gather_edges(read, count_blocks):
+        lanes = lax.broadcasted_iota(jnp.int32, (BLOCK * rows, 128), 1)
+        packed = jnp.zeros((BLOCK * rows, 128), F32)
+        for k in range(count_blocks):
+            block = read(k).reshape(BLOCK * rows, 128)
+            packed = jnp.where(lanes // 2 == k, pltpu.roll(block, (1 + 2 * k) % 128, 1), packed)
+        return packed.T
+
+    def spread(from_e, from_w):
+        tall = from_e.shape[0]
+        odd = lax.rem(lax.broadcasted_iota(jnp.int32, (tall, 128), 0), 2) == 1
+        mixed = jnp.where(odd, pltpu.roll(from_w, 1, 0), pltpu.roll(from_e, tall - 1, 0))
+        if tall < 128:
+            mixed = jnp.concatenate([mixed, jnp.zeros((128 - tall, 128), F32)], axis=0)
+        return mixed.T
+
+    def send_cols(field, k, g):
+        def read(b):
+            return field[
+                g * GROUP + b // parts,
+                pl.ds((b % parts) * BLOCK, BLOCK),
+                pl.ds(TOP, rows),
+                :,
+            ]
+
+        edge[k, g] = gather_edges(read, GROUP * parts)[: edge.shape[2]]
+        for side in (0, 1):
+            col_copy(k, g, side).start()
+
+    @pl.loop(0, chunks)
+    def _(g):
+        send_cols(q0, 0, g)
 
     wload.wait()
 

time: 45.1 us -> 46.1 us (1.022)
  Pallas kernels: 40.5 us -> 41.4 us
    pallas_call x1, Pallas kernels: 40.5 us -> 41.4 us  [per_device(): pl.pallas_call(functools.partial(kernel_body, lat_n, lon_n, tracers, leve...]
where the time goes in v4:
time: 46.1 us; the launch traced here: 45.9 us
  Pallas kernels  41.4 us (90%)
  other arithmetic  3.81 us (8%)
  between operations  0.66 us (1%)
    pallas_call x1, Pallas kernels, per_device(): pl.pallas_call(functools.partial(kernel_body, lat_n, lon_n, tracers, leve...  41.4 us
    add x1, other arithmetic, per_device(): return twice + forced[None]  3.81 us

profile of v4, /device:TPU:0, one launch (start us, length us, event | category | flops | bytes accessed | tf_op | source)
XLA Modules:
  0.0 45.9 jit_solution(11900934905568915825)
XLA Ops:
  0.7 41.4 %shard_map.73 = (f32[16,24,16,128]{3,2,1,0:T(8,128)}, f32[24,16,128]{2,1,0:T(8,128)}) custom-call(f32[16,24,16,128]{3,2,1,0:T(8,128)} %adj.1, f32[2,24,16,128]{3,2,1,0:T(8,128)} %cour.1, f32[24,2048]{1,0:T(8,128)} %kern.1, f32[24]{0:T(128)} %vd.1, s32[1]{0:T(128)S(6)} %copy.8.count, f32[16,128]{1,0:T(8,128)} %bitcast.2, s32[16,128]{1,0:T(8,128)} %bitcast.3), custom_call_target="tpu_custom_call" | custom-call | tf_op jit(solution)/shard_map/pallas_call | solution.py:487
  42.1 3.8 %broadcast_add_fusion = f32[16,24,16,128]{3,2,1,0:T(8,128)} fusion(f32[16,24,16,128]{3,2,1,0:T(8,128)} %get-tuple-element.7, f32[24,16,128]{2,1,0:T(8,128)} %get-tuple-element.8), kind=kLoop, calls=%fused_computation | loop fusion | flops 786432 | bytes 6488064 | tf_op jit(solution)/shard_map/add | solution.py:545
